TPU v7x, 256 devices: a whole 4x4x8 slice. The times are simulated.
256 devices in a mesh: brick: 32 (over z_hi, x, core), view: 8 (over y, z_lo).
Axes of the slice: x: 4, y: 4, z: 8 (z_hi: 4, z_lo: 2; z = z_hi * 2 + z_lo), core: 2. Of those that a mesh axis runs over, the one named last changes fastest.
Arguments:
- estimate: float32 [256, 64, 512], P('brick'), may hold values from 0.5 to 2
- camera_blocks: bfloat16 [8, 512, 8, 2048], P('view', 'brick'), may hold values from 0.099609375 to 2
- block_lists: int32 [8, 32, 32, 2], P('view'), may hold values from -1 to 15, as said below
- block_offsets: int32 [8, 512], P('view'), may hold values from 1 to 252, as said below
- psf_index: int32 [8, 64], P('view'), may hold values from 0 to 15
- psf_bank: float32 [8, 2, 16, 9], P('view'), may hold values from 0.03 to 0.3
Outputs:
- updated: float32 [256, 64, 512], P('brick')
Inputs may be any that keep to these rules, and one draw needn't show every extreme that they name: block_lists[v, d, s] names exactly the blocks of holder s that intersect brick d, each once; at most 2 of them, and 2 for some brick and holder. `block_offsets`: every block starts after its brick's first row by 1 to 4 rows.
All inputs are finite; a program needn't handle non-finite values.
Results may differ from a plain program's by a relative error of at most 0.0003.
Values may be sent and summed in bfloat16 or wider, within the bound.
A program may use at most 128 MiB of HBM per device.

v0:
```python
import jax
import jax.numpy as jnp
from jax import lax
from jax.sharding import PartitionSpec as P


def with_halo(cells, sides, width):
    for axis, dim in sides:
        count = lax.axis_size(axis)
        ends = count - 1
        head = lax.slice_in_dim(cells, 0, width, axis=dim)
        tail = lax.slice_in_dim(cells, cells.shape[dim] - width, cells.shape[dim], axis=dim)
        cells = jnp.concatenate(
            [
                lax.ppermute(tail, axis, [(i, (i + 1) % count) for i in range(ends)]),
                cells,
                lax.ppermute(head, axis, [((i + 1) % count, i) for i in range(ends)]),
            ],
            axis=dim,
        )
    return cells


def joined(value, axis, join):
    pieces = lax.all_gather(value, axis)
    head = pieces[0]
    tail = pieces[1:]
    running, _ = lax.scan(lambda running, slab: (join(running, slab), None), head, tail)
    return running


def blur_cols(field, kern, reverse):
    tap_count = kern.shape[1]
    radius = tap_count // 2
    width = field.shape[2]
    padded = jnp.pad(field, ((0, 0), (0, 0), (radius, radius)))
    result = None
    for offset in range(tap_count):
        begin_at = 2 * radius - offset if reverse else offset
        term = kern[:, offset][None, :, None] * padded[:, :, begin_at : begin_at + width]
        result = term if result is None else result + term
    return result


def blur_rows(padded, kern, reverse, rows):
    tap_count = kern.shape[1]
    radius = tap_count // 2
    result = None
    for offset in range(tap_count):
        begin_at = 2 * radius - offset if reverse else offset
        term = kern[:, offset][None, :, None] * padded[begin_at : begin_at + rows]
        result = term if result is None else result + term
    return result


def place_blocks(blocks, column_ids, row_starts, is_valid, start_x, rows_dev, depth, column_count):
    block_rows = blocks.shape[1]
    block_cols = column_count // 1
    local_rows = row_starts[:, None] + jnp.arange(block_rows, dtype=jnp.int32)[None, :] - start_x
    row_hit = (
        local_rows[:, :, None] == jnp.arange(rows_dev, dtype=jnp.int32)[None, None, :]
    ) & is_valid[:, None, None]
    colhot = column_ids[:, None] == jnp.arange(column_count, dtype=jnp.int32)[None, :]
    weight = (row_hit[:, :, :, None] & colhot[:, None, None, :]).astype(jnp.bfloat16)
    summed = jnp.einsum("sabc,saf->bcf", weight, blocks, preferred_element_type=jnp.float32)
    block_width = blocks.shape[2] // depth
    summed = summed.reshape(rows_dev, block_cols, depth, block_width)
    return summed.transpose(0, 2, 1, 3).reshape(rows_dev, depth, block_cols * block_width)


def multiply(first_value, second_value):
    return first_value * second_value


def shards(estimate, camera_blocks, block_lists, block_offsets, psf_index, psf_bank):
    rows_dev, depth, columns = estimate.shape
    tile_count = camera_blocks.shape[1]
    brick_here = lax.axis_index("brick")
    start_x = brick_here * rows_dev
    tap_count = psf_bank.shape[-1]
    radius = tap_count // 2
    kern_count = psf_bank.shape[2]
    kernel_pick = (
        psf_index[0][:, None] == jnp.arange(kern_count, dtype=jnp.int32)[None, :]
    ).astype(jnp.float32)
    kern_x = jnp.dot(kernel_pick, psf_bank[0, 0], precision=lax.Precision.HIGHEST)
    kern_y = jnp.dot(kernel_pick, psf_bank[0, 1], precision=lax.Precision.HIGHEST)
    offsets_view = block_offsets[0]
    gathered = lax.all_gather(camera_blocks, "brick", axis=1, tiled=True)
    count = gathered.shape[1]
    block_ids = jnp.arange(count, dtype=jnp.int32)
    measured = place_blocks(
        gathered[0],
        block_ids % tile_count,
        offsets_view,
        block_ids >= 0,
        start_x,
        rows_dev,
        depth,
        tile_count,
    )
    padded = with_halo(estimate, (("brick", 0),), radius)
    blurred = blur_rows(blur_cols(padded, kern_y, False), kern_x, False, rows_dev)
    ratio = measured / blurred
    padded_ratio = with_halo(ratio, (("brick", 0),), radius)
    correction = blur_rows(blur_cols(padded_ratio, kern_y, True), kern_x, True, rows_dev)
    product = joined(correction, "view", multiply)
    return estimate * product


def solution(mesh):
    placed = (
        P("brick", None, None),
        P("view", "brick", None, None),
        P("view", None, None, None),
        P("view", None),
        P("view", None),
        P("view", None, None, None),
    )
    return jax.shard_map(
        shards, mesh=mesh, in_specs=placed, out_specs=P("brick", None, None), check_vma=False
    )
```

profile of v0, /device:TPU:8, one launch (start us, length us, event | category | flops | bytes accessed | tf_op | source)
XLA Modules:
  0.0 432.2 jit_solution(10102572551987792969)
XLA Ops:
  7.3 2.1 fusion.49
  9.4 2.5 collective-permute-start
  16.0 1.8 copy.23
  19.3 2.4 copy.24
  21.6 1.6 pad_maximum_fusion
  23.2 6.2 %multiply_add_fusion.1 = f32[16,64,512]{1,2,0:T(8,128)} fusion(f32[16,64,512]{1,2,0:T(8,128)S(1)} %pad_maximum_fusion, f32[64]{0:T(128)S(1)} %get-tuple-element.48, f32[64]{0:T(128)S(1)} %get-tuple-element.49, f32[64]{0:T(128)S(1)} %get-tuple-element.50, f32[64]{0:T(128)S(1)} %get-tuple-element.51, f32[64]{0:T(128)S(1)} %get-tuple-element.52, ...), kind=kLoop, calls=%fused_computation.15 | loop fusion | flops 8912896 | bytes 4196608 | tf_op jit(solution)/shard_map/add | solution.py:41
  29.4 92.2 %all-gather.4.cloned.1.call-done = bf16[1,512,8,2048]{3,2,0,1:T(8,128)(2,1)} async-done(((bf16[1,16,8,2048]{3,2,0,1:T(8,128)(2,1)}), bf16[1,512,8,2048]{3,2,0,1:T(8,128)(2,1)}) %all-gather.4.cloned.1.call-update) | async-done | bytes 16777232 | tf_op jit(solution)/shard_map/all_gather | solution.py:89
  121.6 25.6 %copy.19 = bf16[1,512,8,2048]{1,2,3,0:T(8,128)(2,1)} copy(bf16[1,512,8,2048]{3,2,0,1:T(8,128)(2,1)} %all-gather.4.cloned.1.call-done) | data formatting | bytes 33554432 | tf_op jit(solution)/shard_map/all_gather | solution.py:89
  147.2 29.9 %fusion.32 = f32[8,64,16,32]{1,2,3,0:T(8,128)S(1)} fusion(bf16[64,32,8,512]{3,2,1,0:T(8,128)(2,1)} %bitcast.75, pred[512,16]{0,1:T(8,128)(4,1)S(1)} %iota_compare_fusion.1, pred[512,8,8]{0,1,2:T(8,128)(4,1)S(1)} %iota_compare_fusion), kind=kOutput, calls=%fused_computation.61 | convolution fusion | flops 2148007936 | bytes 17866752 | tf_op jit(solution)/shard_map/sabc,saf->bcf/dot_general | solution.py:65
  177.7 1.5 copy-done
  179.2 1.7 fusion.22
  182.1 2.3 copy.26
  187.0 3.8 collective-permute-start.2
  192.2 2.4 copy.27
  194.6 1.7 pad_maximum_fusion.1
  196.3 5.3 %multiply_add_fusion = f32[16,64,512]{1,2,0:T(8,128)S(1)} fusion(f32[16,64,512]{1,2,0:T(8,128)S(1)} %pad_maximum_fusion.1, f32[64]{0:T(128)S(1)} %get-tuple-element.48, f32[64]{0:T(128)S(1)} %get-tuple-element.49, f32[64]{0:T(128)S(1)} %get-tuple-element.50, f32[64]{0:T(128)S(1)} %get-tuple-element.51, f32[64]{0:T(128)S(1)} %get-tuple-element.52, ...), kind=kLoop, calls=%fused_computation.6 | loop fusion | flops 8912896 | bytes 4196608 | tf_op jit(solution)/shard_map/add | solution.py:41
  202.9 1.6 copy.29
  204.5 201.2 %all-gather.6.cloned.1.call-done = f32[64,64,512]{2,1,0:T(8,128)} async-done(((f32[8,64,512]{2,1,0:T(8,128)}), f32[64,64,512]{2,1,0:T(8,128)}) %all-gather.6.cloned.1.call-update) | async-done | bytes 8388624 | tf_op jit(solution)/shard_map/all_gather | solution.py:25
  405.7 7.7 %slice.301 = f32[56,64,512]{2,1,0:T(8,128)} slice(f32[64,64,512]{2,1,0:T(8,128)} %all-gather.6.cloned.1.call-done), slice={[8:64], [0:64], [0:512]} | slice | bytes 14680064 | tf_op jit(solution)/shard_map/slice | solution.py:27
  413.4 10.7 %while.10 = (s32[]{:T(128)}, f32[8,64,512]{2,1,0:T(8,128)S(1)}, f32[7,8,64,512]{3,2,1,0:T(8,128)}, s32[]{:T(128)}) while((s32[]{:T(128)}, f32[8,64,512]{2,1,0:T(8,128)S(1)}, f32[7,8,64,512]{3,2,1,0:T(8,128)}, s32[]{:T(128)}) %tuple.46), condition=%wide.region_1.2_spmd, body=%wide.region_0.1_spmd.sunk | while | flops 262146 | bytes 3145793 | solution.py:28
  413.4 1.6 bitcast_multiply_fusion.2
  416.5 1.5 bitcast_multiply_fusion.2
  418.0 1.5 bitcast_multiply_fusion.2
  421.1 1.5 bitcast_multiply_fusion.2
  (38 shorter events, 19.0 us)
Async XLA Ops:
  6.5 11.3 %copy-start.2 = (s32[1,512]{1,0:T(1,128)S(1)}, s32[1,512]{1,0:T(1,128)}, u32[]{:S(2)}) copy-start(s32[1,512]{1,0:T(1,128)} %param.10) | copy-start | bytes 6148
  6.5 115.1 %all-gather.4.cloned.1.call-start = ((), (), s32[]{:S(2)}) async-start(), calls=%async_computation | async-start | bytes 17301504 | tf_op jit(solution)/shard_map/all_gather | solution.py:89
  7.3 398.4 %all-gather.6.cloned.1.call-start = ((), (), s32[]{:S(2)}) async-start(), calls=%async_computation.1 | async-start | bytes 9437184 | tf_op jit(solution)/shard_map/all_gather | solution.py:25
  9.4 8.5 %collective-permute-start = (f32[4,64,512]{2,1,0:T(8,128)S(1)}, f32[4,64,512]{2,1,0:T(8,128)}, u32[]{:S(2)}, u32[]{:S(2)}) collective-permute-start(f32[4,64,512]{2,1,0:T(8,128)S(1)} %get-tuple-element.34), channel_id=1, source_target_pairs={{0,8},{8,16},{16,24},{24,32},{32,40},{40,48},{48,56},{56,64},{64,7... | collective-permute-start | bytes 1572872 | tf_op jit(solution)/shard_map/ppermute | solution.py:15
  11.9 7.3 %collective-permute-start.1 = (f32[4,64,512]{2,1,0:T(8,128)}, f32[4,64,512]{2,1,0:T(8,128)}, u32[]{:S(2)}, u32[]{:S(2)}) collective-permute-start(f32[4,64,512]{2,1,0:T(8,128)} %get-tuple-element.35), channel_id=1, source_target_pairs={{8,0},{16,8},{24,16},{32,24},{40,32},{48,40},{56,48},{64,56},{72,6... | collective-permute-start | bytes 1572872 | tf_op jit(solution)/shard_map/ppermute | solution.py:17
  177.1 2.2 copy-start
  184.4 6.4 %collective-permute-start.3 = (f32[4,64,512]{2,1,0:T(8,128)}, f32[4,64,512]{2,1,0:T(8,128)}, u32[]{:S(2)}, u32[]{:S(2)}) collective-permute-start(f32[4,64,512]{2,1,0:T(8,128)} %copy.26), channel_id=1, source_target_pairs={{8,0},{16,8},{24,16},{32,24},{40,32},{48,40},{56,48},{64,56},{72,6... | collective-permute-start | bytes 1572872 | tf_op jit(solution)/shard_map/ppermute | solution.py:17
  187.0 5.2 %collective-permute-start.2 = (f32[4,64,512]{2,1,0:T(8,128)}, f32[4,64,512]{2,1,0:T(8,128)}, u32[]{:S(2)}, u32[]{:S(2)}) collective-permute-start(f32[4,64,512]{2,1,0:T(8,128)} %copy.25), channel_id=1, source_target_pairs={{0,8},{8,16},{16,24},{24,32},{32,40},{40,48},{48,56},{56,64},{64,7... | collective-permute-start | bytes 1572872 | tf_op jit(solution)/shard_map/ppermute | solution.py:15
  405.7 7.7 %slice-start = ((f32[64,64,512]{2,1,0:T(8,128)}), f32[8,64,512]{2,1,0:T(8,128)S(1)}, s32[]{:S(2)}) async-start(f32[64,64,512]{2,1,0:T(8,128)} %all-gather.6.cloned.1.call-done), calls=%async_computation.2 | async-start | bytes 2097152 | tf_op jit(solution)/shard_map/slice | solution.py:26
  413.4 10.7 %copy-start.1 = (f32[8,64,512]{2,1,0:T(8,128)S(1)}, f32[8,64,512]{2,1,0:T(8,128)}, u32[]{:S(2)}) copy-start(f32[8,64,512]{2,1,0:T(8,128)} %param.8) | copy-start | bytes 3145732
Sparse Core Ops, SparseCore 0:
  9.9 111.6 all-gather.3
  204.6 201.0 all-gather.5
where the time goes:
time: 435 us; the launch traced here: 432 us
  waiting for transfers between devices  294 us (68%)
  local copies, waits for them, and re-layouts  53.9 us (12%)
  matrix products  31.6 us (7%)
  other arithmetic  29.6 us (7%)
  between operations  13.6 us (3%)
  starting transfers between devices  9.15 us (2%)
    all_gather x1, waiting for transfers between devices, joined(): pieces = lax.all_gather(value, axis)  201 us
    all_gather x1, waiting for transfers between devices, shards(): gathered = lax.all_gather(camera_blocks, 'brick', axis=1, tiled=True)  92.2 us
    dot_general x1, matrix products, place_blocks(): jnp.einsum('sabc,saf->bcf', weight, blocks, preferred_element_type=jnp.fl...  29.9 us
    all_gather x1, local copies, waits for them, and re-layouts, shards(): gathered = lax.all_gather(camera_blocks, 'brick', axis=1, tiled=True)  25.6 us
    add x2, other arithmetic, blur_cols(): result = term if result is None else result + term  11.4 us
    mul x7, other arithmetic, multiply(): return first_value * second_value  10.6 us
  transfers between devices with their start and end apart: 6, of which 2 were waited for; matrix products, arithmetic and copies ran while one was open for 5% of the time, Pallas kernels for 0%

commit v1 on v0

v1 whole, which is shorter than its diff:
```python
import functools

import jax
import jax.numpy as jnp
from jax import lax
from jax.experimental import pallas as pl
from jax.experimental.pallas import tpu as pltpu
from jax.sharding import PartitionSpec as P

F32 = jnp.float32
BF16 = jnp.bfloat16
MESH = pl.DeviceIdType.MESH
TAPS = 9
RAD = TAPS // 2
ROWS = 256
GROUPS = 4
PAD = 8
META = 56


def column_pass(parts, tap, reverse):
    lane = lax.broadcasted_iota(jnp.int32, (8, 128), 1)
    sums = [tap(RAD) * part for part in parts]
    for shift in range(-RAD, RAD + 1):
        if shift == 0:
            continue
        weight = tap(RAD - shift if reverse else RAD + shift)
        turned = [pltpu.roll(part, (-shift) % 128, 1) for part in parts]
        keep = lane < 128 - shift if shift > 0 else lane >= -shift
        for g in range(GROUPS):
            other = g + 1 if shift > 0 else g - 1
            beside = turned[other] if 0 <= other < GROUPS else jnp.zeros((8, 128), F32)
            sums[g] = sums[g] + weight * jnp.where(keep, turned[g], beside)
    return sums


def row_pass(load, tap, reverse):
    total = None
    for shift in range(-RAD, RAD + 1):
        weight = tap(RAD - shift if reverse else RAD + shift)
        term = weight * load(shift)
        total = term if total is None else total + term
    return total


def swap_lanes(low, high, width, keep):
    new_low = jnp.where(keep, low, pltpu.roll(high, width, 1))
    new_high = jnp.where(keep, pltpu.roll(low, 128 - width, 1), high)
    return new_low, new_high


def kernel(
    est_ref, cam_ref, table_ref, index_ref, bank_ref, out_ref,
    cam_t, cam_r, est_t, est_r, meta_s, meta_r, taps, onehot, blurred, ratio, part, other, back,
    s_est, r_est, s_fwd, r_fwd, s_meta, r_meta, s_cam, r_cam, s_half, r_half, s_back, r_back, s_out, r_out,
):
    brick = lax.axis_index("brick")
    view = lax.axis_index("view")
    zh, x, c = brick // 8, (brick // 2) % 4, brick % 2
    y, zl = view // 2, view % 2
    core_of_y = y // 2
    half_of_zh = zh // 2

    def place(zh_, x_, c_, y_, zl_):
        return (zh_ * 8 + x_ * 2 + c_, y_ * 2 + zl_)

    barrier = pltpu.get_barrier_semaphore()

    def greet(target):
        pl.semaphore_signal(barrier, inc=1, device_id=target, device_id_type=MESH)

    @pl.loop(0, 64)
    def _(i):
        zh_, x_, c_, yy = i // 16, (i // 4) % 4, (i // 2) % 2, 2 * c + i % 2
        target = place(zh_, x_, c_, yy, zl)

        @pl.when(jnp.logical_not((zh_ == zh) & (x_ == x) & (c_ == c) & (yy == y)))
        def _():
            greet(target)

    @pl.loop(1, 16)
    def _(i):
        greet(place((zh + i // 4) % 4, (x + i % 4) % 4, c, y, zl))

    greet(place(zh, x, 1 - c, y, zl))

    @pl.loop(0, 32)
    def _(i):
        zh_, x_, zl_ = i // 8, (i // 2) % 4, i % 2

        @pl.when(jnp.logical_not((zh_ == zh) & (x_ == x) & (zl_ == zl) & (half_of_zh == c)))
        def _():
            greet(place(zh_, x_, half_of_zh, y, zl_))

    @pl.loop(1, 8)
    def _(i):
        greet((brick, (view + i) % 8))

    lane = lax.broadcasted_iota(jnp.int32, (8, 128), 1)
    for g in range(GROUPS):
        cells = est_ref[:, pl.ds(pl.multiple_of(16 * y, 16), 16), g * 128:(g + 1) * 128]
        est_t[:, g] = jnp.transpose(cells, (1, 0, 2))
        est_r[g, 0:PAD, :] = jnp.zeros((PAD, 128), F32)
        est_r[g, PAD + ROWS:, :] = jnp.zeros((PAD, 128), F32)
        for w in range(2):
            ratio[w, g, 0:PAD, :] = jnp.zeros((PAD, 128), F32)
            ratio[w, g, PAD + ROWS:, :] = jnp.zeros((PAD, 128), F32)
    for k in range(4):
        kern = index_ref[0, 16 * k + zh * 4 + x]
        for a in range(2):
            for q in range(TAPS):
                meta_s[k, a * TAPS + q:a * TAPS + q + 1, :] = jnp.full((1, 128), bank_ref[0, a, kern, q], F32)
        meta_s[k, 24:META, :] = table_ref[...]

    same = (core_of_y == c).astype(jnp.int32)
    back_same = (half_of_zh == c).astype(jnp.int32)
    pl.semaphore_wait(barrier, (64 - same) + 15 + 1 + (32 - back_same) + 7)

    @pl.loop(1, 16)
    def _(i):
        zh_, x_ = (zh + i // 4) % 4, (x + i % 4) % 4
        pltpu.make_async_remote_copy(
            est_t.at[zh_ * 4 + x_], est_r.at[:, pl.ds(pl.multiple_of(PAD + 8 * brick, 8), 8), :], s_est, r_est,
            device_id=place(zh_, x_, c, y, zl), device_id_type=MESH,
        ).start()

    pltpu.make_async_copy(
        est_t.at[zh * 4 + x], est_r.at[:, pl.ds(pl.multiple_of(PAD + 8 * brick, 8), 8), :], r_est
    ).start()

    @pl.when(core_of_y == c)
    def _():
        @pl.loop(1, 4)
        def _(i):
            y_ = (y + i) % 4
            pltpu.make_async_remote_copy(
                meta_s.at[y_], meta_r.at[y % 2], s_meta, r_meta,
                device_id=place(zh, x, c, y_, zl), device_id_type=MESH,
            ).start()

    @pl.when(core_of_y == c)
    def _():
        pltpu.make_async_copy(meta_s.at[y], meta_r.at[y % 2], r_meta).start()

    upper = lane < 64
    lower = (lane // 32) % 2 == 0

    @pl.loop(0, 16)
    def _(i):
        y_, zh_ = (y + i // 4) % 4, (zh + i % 4) % 4
        quad = y_ * 4 + zh_
        start = pl.multiple_of(quad * 128, 128)
        for g in range(2):
            turned = []
            for h in range(2):
                v = [cam_ref[0, h * 8 + g * 4 + n, :, pl.ds(start, 128)].astype(F32) for n in range(4)]
                v[0], v[2] = swap_lanes(v[0], v[2], 64, upper)
                v[1], v[3] = swap_lanes(v[1], v[3], 64, upper)
                v[0], v[1] = swap_lanes(v[0], v[1], 32, lower)
                v[2], v[3] = swap_lanes(v[2], v[3], 32, lower)
                turned.append(v)
            for n in range(4):
                pair = jnp.concatenate([turned[0][n], turned[1][n]], axis=0).astype(BF16)
                cam_t[quad * 4 + n, :, g * 128:(g + 1) * 128] = pair

        @pl.loop(0, 4)
        def _(n):
            x_ = (x + n) % 4
            depth = quad * 4 + x_
            here = (y_ == y) & (zh_ == zh) & (x_ == x) & (core_of_y == c)

            @pl.when(jnp.logical_not(here))
            def _():
                pltpu.make_async_remote_copy(
                    cam_t.at[depth], cam_r.at[y % 2, brick], s_cam, r_cam,
                    device_id=place(zh_, x_, core_of_y, y_, zl), device_id_type=MESH,
                ).start()

            @pl.when(here)
            def _():
                pltpu.make_async_copy(cam_t.at[depth], cam_r.at[y % 2, brick], r_cam).start()

    pltpu.make_async_copy(est_r.at[:, 8:136, :], est_r.at[:, 8:136, :], r_est).wait()

    @pl.loop(0, 16)
    def _(i):
        rows = pl.ds(pl.multiple_of(PAD + 8 * (2 * i + c), 8), 8)
        pltpu.make_async_remote_copy(
            est_r.at[:, rows, :], est_r.at[:, rows, :], s_fwd, r_fwd,
            device_id=place(zh, x, 1 - c, y, zl), device_id_type=MESH,
        ).start()

    pltpu.make_async_copy(meta_r, meta_r, r_meta).wait()
    row_id = lax.broadcasted_iota(jnp.int32, (ROWS, 128), 0).astype(F32)
    for w in range(2):
        for q in range(2 * TAPS):
            taps[w, q] = jnp.broadcast_to(meta_r[w, q:q + 1, :], (8, 128))

        @pl.loop(0, GROUPS)
        def _(g):
            for n in range(4):
                for k in range(2):
                    starts = meta_r[w, pl.ds(24 + (g * 4 + n) * 2 + k, 1), :]
                    hit = jnp.where(row_id == starts, 1.0, 0.0).astype(BF16)
                    onehot[w, g, :, n * 256 + k * 128:n * 256 + (k + 1) * 128] = hit

    pltpu.make_async_copy(est_r.at[:, 8:136, :], est_r.at[:, 8:136, :], r_fwd).wait()

    @pl.loop(0, ROWS // 8)
    def _(i):
        row = pl.multiple_of(8 * i, 8)
        for w in range(2):
            parts = [
                row_pass(lambda s, g=g: est_r[g, pl.ds(row + (PAD + s), 8), :], lambda q: taps[w, q], False)
                for g in range(GROUPS)
            ]
            sums = column_pass(parts, lambda q: taps[w, TAPS + q], False)
            for g in range(GROUPS):
                blurred[w, g, pl.ds(row, 8), :] = sums[g]

    pltpu.make_async_copy(cam_r, cam_r, r_cam).wait()
    block_lane = lax.broadcasted_iota(jnp.int32, (ROWS, 128), 1) // 32

    @pl.loop(0, 2)
    def _(w):
        for g in range(GROUPS):
            h = g // 2
            cells = cam_r[w, :, :, (g % 2) * 128:(g % 2 + 1) * 128].astype(F32)
            cells = cells[:, h * 8:(h + 1) * 8, :].reshape(ROWS, 128)
            stack = jnp.concatenate(
                [jnp.where(block_lane == n, cells, 0.0).astype(BF16) for n in range(4)], axis=0
            )
            measured = jnp.dot(onehot[w, g], stack, preferred_element_type=F32)
            ratio[w, g, PAD:PAD + ROWS, :] = measured / blurred[w, g]

    def correct(first):
        @pl.loop(0, 16)
        def _(i):
            row = pl.multiple_of(first + 8 * i, 8)
            product = None
            for w in range(2):
                parts = [
                    row_pass(lambda s, g=g: ratio[w, g, pl.ds(row + (PAD + s), 8), :], lambda q: taps[w, q], True)
                    for g in range(GROUPS)
                ]
                sums = column_pass(parts, lambda q: taps[w, TAPS + q], True)
                product = sums if product is None else [a * b for a, b in zip(product, sums)]
            for g in range(GROUPS):
                part[g, pl.ds(row, 8), :] = product[g]

    correct((1 - c) * 128)
    theirs = part.at[:, pl.ds(pl.multiple_of((1 - c) * 128, 128), 128), :]
    half = pltpu.make_async_remote_copy(
        theirs, other, s_half, r_half, device_id=place(zh, x, 1 - c, y, zl), device_id_type=MESH
    )
    half.start()
    correct(c * 128)
    half.wait()
    mine = pl.ds(pl.multiple_of(c * 128, 128), 128)
    for g in range(GROUPS):
        other[g] = other[g] * part[g, mine, :]

    @pl.loop(0, 32)
    def _(i):
        slot, h = i // 2, i % 2
        target = 16 * c + slot
        here = (target == brick) & (h == zl)
        source = other.at[pl.ds(2 * h, 2), pl.ds(pl.multiple_of(8 * slot, 8), 8), :]

        @pl.when(jnp.logical_not(here))
        def _():
            pltpu.make_async_remote_copy(
                source, back.at[zl, zh * 4 + x], s_back, r_back,
                device_id=(target, y * 2 + h), device_id_type=MESH,
            ).start()

        @pl.when(here)
        def _():
            pltpu.make_async_copy(source, back.at[zl, zh * 4 + x], r_back).start()

    pltpu.make_async_copy(back, back, r_back).wait()
    depths = pl.ds(pl.multiple_of(16 * y, 16), 16)
    for k in range(2):
        columns = pl.ds(pl.multiple_of(zl * 256 + k * 128, 128), 128)
        both = back[0, :, k] * back[1, :, k]
        out_ref[:, depths, columns] = jnp.transpose(both, (1, 0, 2)) * est_ref[:, depths, columns]

    piece = out_ref.at[:, depths, pl.ds(pl.multiple_of(zl * 256, 256), 256)]

    @pl.loop(1, 8)
    def _(i):
        pltpu.make_async_remote_copy(
            piece, piece, s_out, r_out, device_id=(brick, (view + i) % 8), device_id_type=MESH
        ).start()

    pltpu.make_async_copy(out_ref.at[0:7], out_ref.at[0:7], r_out).wait()
    pltpu.make_async_copy(out_ref.at[0:7], out_ref.at[0:7], s_out).wait()

    sent = est_r.at[:, 8:128, :]
    pltpu.make_async_copy(sent, sent, s_est).wait()
    pltpu.make_async_copy(est_r.at[:, 8:136, :], est_r.at[:, 8:136, :], s_fwd).wait()

    @pl.when(core_of_y == c)
    def _():
        pltpu.make_async_copy(meta_s.at[0:3], meta_s.at[0:3], s_meta).wait()
        pltpu.make_async_copy(cam_t.at[0:63], cam_t.at[0:63], s_cam).wait()

    @pl.when(core_of_y != c)
    def _():
        pltpu.make_async_copy(cam_t, cam_t, s_cam).wait()

    @pl.when(half_of_zh == c)
    def _():
        pltpu.make_async_copy(back.at[0, 0:15], back.at[0, 0:15], s_back).wait()
        pltpu.make_async_copy(back.at[1], back.at[1], s_back).wait()

    @pl.when(half_of_zh != c)
    def _():
        pltpu.make_async_copy(back, back, s_back).wait()


def shards(estimate, camera_blocks, block_lists, block_offsets, psf_index, psf_bank):
    starts = block_offsets[0].reshape(32, 16).T
    table = starts[:, :, None] + jnp.arange(8, dtype=jnp.int32)[None, None, :]
    table = table.reshape(32, 128).astype(F32)
    vmem = pl.BlockSpec(memory_space=pltpu.VMEM)
    smem = pl.BlockSpec(memory_space=pltpu.SMEM)
    dma = pltpu.SemaphoreType.DMA
    return pl.pallas_call(
        kernel,
        out_shape=jax.ShapeDtypeStruct(estimate.shape, F32),
        in_specs=[vmem, vmem, vmem, smem, smem],
        out_specs=vmem,
        scratch_shapes=[
            pltpu.VMEM((64, 16, 256), BF16),
            pltpu.VMEM((2, 32, 16, 256), BF16),
            pltpu.VMEM((16, GROUPS, 8, 128), F32),
            pltpu.VMEM((GROUPS, ROWS + 2 * PAD, 128), F32),
            pltpu.VMEM((4, META, 128), F32),
            pltpu.VMEM((2, META, 128), F32),
            pltpu.VMEM((2, 2 * TAPS, 8, 128), F32),
            pltpu.VMEM((2, GROUPS, ROWS, 1024), BF16),
            pltpu.VMEM((2, GROUPS, ROWS, 128), F32),
            pltpu.VMEM((2, GROUPS, ROWS + 2 * PAD, 128), F32),
            pltpu.VMEM((GROUPS, ROWS, 128), F32),
            pltpu.VMEM((GROUPS, 128, 128), F32),
            pltpu.VMEM((2, 16, 2, 8, 128), F32),
        ] + [dma] * 14,
        compiler_params=pltpu.CompilerParams(
            collective_id=0, has_side_effects=True, vmem_limit_bytes=40 * 1024 * 1024
        ),
        cost_estimate=pl.CostEstimate(flops=600_000_000, bytes_accessed=4_000_000, transcendentals=0),
    )(estimate, camera_blocks, table, psf_index, psf_bank)


def solution(mesh):
    placed = (
        P("brick", None, None),
        P("view", "brick", None, None),
        P("view", None, None, None),
        P("view", None),
        P("view", None),
        P("view", None, None, None),
    )
    return jax.shard_map(
        shards, mesh=mesh, in_specs=placed, out_specs=P("brick", None, None), check_vma=False
    )
```

time: 435 us -> 70.6 us (0.16)
  the two profiles are of different devices: /device:TPU:8 before, /device:TPU:1 now
where the time goes in v1:
time: 70.6 us; the launch traced here: 70.4 us
  Pallas kernels  64.6 us (92%)
  local copies, waits for them, and re-layouts  4.29 us (6%)
  other arithmetic  1.47 us (2%)
    pallas_call x1, Pallas kernels, shards(): pl.pallas_call(kernel, out_shape=jax.ShapeDtypeStruct(estimate.shape, F32...  64.6 us
    unnamed x9, local copies, waits for them, and re-layouts  3.99 us

profile of v1, /device:TPU:1, one launch (start us, length us, event | category | flops | bytes accessed | tf_op | source)
XLA Modules:
  0.0 70.4 jit_solution(8667516792454374929)
XLA Ops:
  0.0 0.0 copy-start.1
  0.0 0.5 broadcast.6
  0.5 1.3 %reduce.3 = s32[512]{0:T(512)S(1)} reduce(s32[1,512]{1,0:T(1,128)} %param.8, s32[]{:T(128)} %broadcast.6), dimensions={0}, to_apply=%param.8.reduce_sub_computation.3 | reduce | bytes 4100 | tf_op args[3]
  1.9 0.1 reshape_squeeze.3
  1.9 0.1 copy.8
  2.0 0.8 %copy.9.bank_ref = f32[1,2,16,9]{3,2,1,0:T(8,128)S(1)} copy(f32[1,2,16,9]{2,1,3,0:T(2,128)} %param.10) | data formatting | bytes 2304 | tf_op args[5]
  2.8 0.1 add_convert_fusion
  2.9 0.0 copy-start.2
  2.9 0.1 convert_element_type.6.table_ref
  3.1 0.0 copy-done.1
  3.1 0.5 copy-done.2
  3.6 0.0 copy-start
  3.6 1.2 %copy-done = f32[8,64,512]{2,1,0:T(8,128)S(1)} copy-done((f32[8,64,512]{2,1,0:T(8,128)S(1)}, f32[8,64,512]{2,1,0:T(8,128)}, u32[]{:S(2)}) %copy-start) | copy-done | bytes 1048600
  4.8 64.6 %shard_map.55 = f32[8,64,512]{2,1,0:T(8,128)S(1)} custom-call(f32[8,64,512]{2,1,0:T(8,128)S(1)} %copy-done, bf16[1,16,8,2048]{3,2,1,0:T(8,128)(2,1)S(1)} %copy-done.1, f32[32,128]{1,0:T(8,128)S(1)} %convert_element_type.6.table_ref, s32[1,64]{1,0:T(1,128)S(1)} %copy-done.2, f32[1,2,16,9]{3,2,1,0:T(8,128)S(1)} %copy.9.bank_ref), custom_call_target="tpu_custom_call" | custom-call | flops 600000000 | bytes 4000000 | tf_op jit(solution)/shard_map/pallas_call | solution.py:329
  69.5 1.0 %copy.11 = f32[8,64,512]{2,1,0:T(8,128)} copy(f32[8,64,512]{2,1,0:T(8,128)S(1)} %shard_map.55) | data formatting | bytes 2097152
Async XLA Ops:
  0.0 3.1 %copy-start.1 = (bf16[1,16,8,2048]{3,2,1,0:T(8,128)(2,1)S(1)}, bf16[1,16,8,2048]{3,2,1,0:T(8,128)(2,1)}, u32[]{:S(2)}) copy-start(bf16[1,16,8,2048]{3,2,1,0:T(8,128)(2,1)} %cam_ref.1) | copy-start | bytes 1572868
  2.9 0.7 copy-start.2
  3.6 1.2 %copy-start = (f32[8,64,512]{2,1,0:T(8,128)S(1)}, f32[8,64,512]{2,1,0:T(8,128)}, u32[]{:S(2)}) copy-start(f32[8,64,512]{2,1,0:T(8,128)} %est_ref.1) | copy-start | bytes 3145732

commit v2 on v1

v2 whole, which is shorter than its diff:
```python
import functools

import jax
import jax.numpy as jnp
from jax import lax
from jax.experimental import pallas as pl
from jax.experimental.pallas import tpu as pltpu
from jax.sharding import PartitionSpec as P

F32 = jnp.float32
BF16 = jnp.bfloat16
MESH = pl.DeviceIdType.MESH
TAPS = 9
RAD = TAPS // 2
ROWS = 256
GROUPS = 4
PAD = 8
META = 24


def column_pass(parts, tap, reverse):
    lane = lax.broadcasted_iota(jnp.int32, (8, 128), 1)
    sums = [tap(RAD) * part for part in parts]
    for shift in range(-RAD, RAD + 1):
        if shift == 0:
            continue
        weight = tap(RAD - shift if reverse else RAD + shift)
        turned = [pltpu.roll(part, (-shift) % 128, 1) for part in parts]
        keep = lane < 128 - shift if shift > 0 else lane >= -shift
        for g in range(GROUPS):
            other = g + 1 if shift > 0 else g - 1
            beside = turned[other] if 0 <= other < GROUPS else jnp.zeros((8, 128), F32)
            sums[g] = sums[g] + weight * jnp.where(keep, turned[g], beside)
    return sums


def row_pass(load, tap, reverse):
    total = None
    for shift in range(-RAD, RAD + 1):
        weight = tap(RAD - shift if reverse else RAD + shift)
        term = weight * load(shift)
        total = term if total is None else total + term
    return total


def swap_lanes(low, high, width, keep):
    new_low = jnp.where(keep, low, pltpu.roll(high, width, 1))
    new_high = jnp.where(keep, pltpu.roll(low, 128 - width, 1), high)
    return new_low, new_high


def kernel(
    est_hbm, cam_hbm, starts_hbm, index_hbm, bank_hbm, out_ref,
    est_ref, cam_ref, starts_ref, index_ref, bank_ref,
    cam_t, cam_r, est_t, est_r, meta_s, meta_r, table, taps, onehot, blurred, ratio, part, other, back,
    s_load, s_est, r_est, s_fwd, r_fwd, s_meta, r_meta, s_cam, r_cam, s_half, r_half, s_back, r_back, s_out, r_out,
):
    brick = lax.axis_index("brick")
    view = lax.axis_index("view")
    zh, x, c = brick // 8, (brick // 2) % 4, brick % 2
    y, zl = view // 2, view % 2
    over = 1 - zl
    step = 2 * zl + 3
    core_of_y = y // 2
    half_of_zh = zh // 2

    loads = [
        pltpu.make_async_copy(source, target, s_load.at[n])
        for n, (source, target) in enumerate(
            [(est_hbm, est_ref), (index_hbm, index_ref), (bank_hbm, bank_ref), (starts_hbm, starts_ref), (cam_hbm, cam_ref)]
        )
    ]
    for load in loads:
        load.start()

    def place(zh_, x_, c_, y_, zl_):
        return (zh_ * 8 + x_ * 2 + c_, y_ * 2 + zl_)

    barrier = pltpu.get_barrier_semaphore()

    def greet(target):
        pl.semaphore_signal(barrier, inc=1, device_id=target, device_id_type=MESH)

    @pl.loop(0, 64)
    def _(i):
        greet(place((zh + i // 16) % 4, (x + i // 4) % 4, (i // 2) % 2, 2 * c + i % 2, over))

    def target_of(m):
        shift = jnp.where(m == 0, 0, jnp.where(m == 3, 2, step))
        return (zh + shift) % 4, jnp.where(m % 2 == 0, zl, over)

    def source_of(m):
        shift = jnp.where(m == 2, 8 - step, jnp.where(m == 1, step, jnp.where(m == 3, 2, 0)))
        return (zh + shift) % 4, jnp.where(m % 2 == 0, zl, over)

    @pl.loop(1, 16)
    def _(i):
        zh_, zl_ = source_of(i // 4)
        greet(place(zh_, (x + i % 4) % 4, c, y, zl_))

    @pl.loop(0, 32)
    def _(i):
        zh_, x_, zl_ = i // 8, (i // 2) % 4, i % 2

        @pl.when(jnp.logical_not((zh_ == zh) & (x_ == x) & (zl_ == zl) & (half_of_zh == c)))
        def _():
            greet(place(zh_, x_, half_of_zh, y, zl_))

    partner = place(zh, x, 1 - c, y, zl)
    ahead = (brick, ((y + 1) % 4) * 2 + zl)
    behind = (brick, ((y + 3) % 4) * 2 + zl)
    across = (brick, y * 2 + over)
    for target in (partner, ahead, behind, across):
        greet(target)

    lane = lax.broadcasted_iota(jnp.int32, (8, 128), 1)
    for g in range(GROUPS):
        est_r[g, 0:PAD, :] = jnp.zeros((PAD, 128), F32)
        est_r[g, PAD + ROWS:, :] = jnp.zeros((PAD, 128), F32)
        for w in range(2):
            ratio[w, g, 0:PAD, :] = jnp.zeros((PAD, 128), F32)
            ratio[w, g, PAD + ROWS:, :] = jnp.zeros((PAD, 128), F32)
    loads[0].wait()
    for g in range(GROUPS):
        cells = est_ref[:, pl.ds(pl.multiple_of(16 * y, 16), 16), g * 128:(g + 1) * 128]
        est_t[:, g] = jnp.transpose(cells, (1, 0, 2))
    for load in loads[1:4]:
        load.wait()
    for k in range(4):
        kern = index_ref[0, 16 * k + zh * 4 + x]
        for a in range(2):
            for q in range(TAPS):
                meta_s[k, a * TAPS + q:a * TAPS + q + 1, :] = jnp.full((1, 128), bank_ref[q, a, kern], F32)
        for n in range(4):
            meta_s[k, 20 + n:21 + n, :] = starts_ref[:, n * 128:(n + 1) * 128].astype(F32)

    back_same = (half_of_zh == c).astype(jnp.int32)
    pl.semaphore_wait(barrier, 64 + 15 + (32 - back_same) + 4)
    own_rows = pl.ds(pl.multiple_of(PAD + 8 * brick, 8), 8)

    @pl.loop(0, 15)
    def _(n):
        i = 15 - n
        zh_, zl_ = target_of(i // 4)
        x_ = (x + i % 4) % 4
        pltpu.make_async_remote_copy(
            est_t.at[zh_ * 4 + x_], est_r.at[:, own_rows, :], s_est, r_est,
            device_id=place(zh_, x_, c, y, zl_), device_id_type=MESH,
        ).start()

    pltpu.make_async_copy(est_t.at[zh * 4 + x], est_r.at[:, own_rows, :], r_est).start()

    @pl.when(core_of_y == c)
    def _():
        @pl.loop(0, 4)
        def _(i):
            y_ = (y + i) % 4
            pltpu.make_async_remote_copy(
                meta_s.at[y_], meta_r.at[y % 2], s_meta, r_meta,
                device_id=place(zh, x, c, y_, over), device_id_type=MESH,
            ).start()

    loads[4].wait()
    upper = lane < 64
    lower = (lane // 32) % 2 == 0

    @pl.loop(0, 16)
    def _(i):
        y_, zh_ = (y + i // 4) % 4, (zh + i % 4) % 4
        quad = y_ * 4 + zh_
        start = pl.multiple_of(quad * 128, 128)
        for g in range(2):
            turned = []
            for h in range(2):
                v = [cam_ref[0, h * 8 + g * 4 + n, :, pl.ds(start, 128)].astype(F32) for n in range(4)]
                v[0], v[2] = swap_lanes(v[0], v[2], 64, upper)
                v[1], v[3] = swap_lanes(v[1], v[3], 64, upper)
                v[0], v[1] = swap_lanes(v[0], v[1], 32, lower)
                v[2], v[3] = swap_lanes(v[2], v[3], 32, lower)
                turned.append(v)
            for n in range(4):
                pair = jnp.concatenate([turned[0][n], turned[1][n]], axis=0).astype(BF16)
                cam_t[quad * 4 + n, :, g * 128:(g + 1) * 128] = pair

        @pl.loop(0, 4)
        def _(n):
            x_ = (x + n) % 4
            depth = quad * 4 + x_
            pltpu.make_async_remote_copy(
                cam_t.at[depth], cam_r.at[y % 2, brick], s_cam, r_cam,
                device_id=place(zh_, x_, core_of_y, y_, over), device_id_type=MESH,
            ).start()

    pltpu.make_async_copy(est_r.at[:, 8:136, :], est_r.at[:, 8:136, :], r_est).wait()

    @pl.loop(0, 16)
    def _(i):
        rows = pl.ds(pl.multiple_of(PAD + 8 * (2 * i + c), 8), 8)
        pltpu.make_async_remote_copy(
            est_r.at[:, rows, :], est_r.at[:, rows, :], s_fwd, r_fwd,
            device_id=partner, device_id_type=MESH,
        ).start()

    pltpu.make_async_copy(meta_r, meta_r, r_meta).wait()
    row_id = lax.broadcasted_iota(jnp.int32, (ROWS, 128), 0).astype(F32)
    block = lax.broadcasted_iota(jnp.int32, (16, 512), 1)
    tile = lax.broadcasted_iota(jnp.int32, (16, 512), 0)
    holder = lax.broadcasted_iota(jnp.int32, (512, 256), 0) // 16
    owner = lax.broadcasted_iota(jnp.int32, (512, 256), 1) // 8
    spread = jnp.where(holder == owner, 1.0, 0.0).astype(BF16)
    inside = (lax.broadcasted_iota(jnp.int32, (16, 256), 1) % 8).astype(F32)
    for w in range(2):
        for q in range(2 * TAPS):
            taps[w, q] = jnp.broadcast_to(meta_r[w, q:q + 1, :], (8, 128))
        starts = jnp.concatenate([meta_r[w, 20 + n:21 + n, :] for n in range(4)], axis=1)
        by_tile = jnp.where(block % 16 == tile, jnp.broadcast_to(starts, (16, 512)), 0.0).astype(BF16)
        rows_of = jnp.dot(by_tile, spread, preferred_element_type=F32) + inside
        for k in range(2):
            table[w, k] = rows_of[:, k * 128:(k + 1) * 128]

        @pl.loop(0, GROUPS)
        def _(g):
            for n in range(4):
                for k in range(2):
                    first = table[w, k, pl.ds(g * 4 + n, 1), :]
                    hit = jnp.where(row_id == first, 1.0, 0.0).astype(BF16)
                    onehot[w, g, :, n * 256 + k * 128:n * 256 + (k + 1) * 128] = hit

    pltpu.make_async_copy(est_r.at[:, 8:136, :], est_r.at[:, 8:136, :], r_fwd).wait()

    @pl.loop(0, ROWS // 8)
    def _(i):
        row = pl.multiple_of(8 * i, 8)
        for w in range(2):
            parts = [
                row_pass(lambda s, g=g: est_r[g, pl.ds(row + (PAD + s), 8), :], lambda q: taps[w, q], False)
                for g in range(GROUPS)
            ]
            sums = column_pass(parts, lambda q: taps[w, TAPS + q], False)
            for g in range(GROUPS):
                blurred[w, g, pl.ds(row, 8), :] = sums[g]

    pltpu.make_async_copy(cam_r, cam_r, r_cam).wait()
    block_lane = lax.broadcasted_iota(jnp.int32, (ROWS, 128), 1) // 32

    @pl.loop(0, 2)
    def _(w):
        for g in range(GROUPS):
            h = g // 2
            cells = cam_r[w, :, :, (g % 2) * 128:(g % 2 + 1) * 128].astype(F32)
            cells = cells[:, h * 8:(h + 1) * 8, :].reshape(ROWS, 128)
            stack = jnp.concatenate(
                [jnp.where(block_lane == n, cells, 0.0).astype(BF16) for n in range(4)], axis=0
            )
            measured = jnp.dot(onehot[w, g], stack, preferred_element_type=F32)
            ratio[w, g, PAD:PAD + ROWS, :] = measured / blurred[w, g]

    def correct(first):
        @pl.loop(0, 16)
        def _(i):
            row = pl.multiple_of(first + 8 * i, 8)
            product = None
            for w in range(2):
                parts = [
                    row_pass(lambda s, g=g: ratio[w, g, pl.ds(row + (PAD + s), 8), :], lambda q: taps[w, q], True)
                    for g in range(GROUPS)
                ]
                sums = column_pass(parts, lambda q: taps[w, TAPS + q], True)
                product = sums if product is None else [a * b for a, b in zip(product, sums)]
            for g in range(GROUPS):
                part[g, pl.ds(row, 8), :] = product[g]

    correct((1 - c) * 128)
    theirs = part.at[:, pl.ds(pl.multiple_of((1 - c) * 128, 128), 128), :]
    half = pltpu.make_async_remote_copy(
        theirs, other, s_half, r_half, device_id=partner, device_id_type=MESH
    )
    half.start()
    correct(c * 128)
    half.wait()

    @pl.loop(0, 16)
    def _(i):
        slot = (brick + i) % 16
        target = 16 * c + slot
        rows = pl.ds(pl.multiple_of(8 * slot, 8), 8)
        here_rows = pl.ds(pl.multiple_of(c * 128 + 8 * slot, 8), 8)
        other[:, rows, :] = other[:, rows, :] * part[:, here_rows, :]
        for h in range(2):
            here = (target == brick) & (h == zl)
            source = other.at[2 * h:2 * h + 2, rows, :]

            @pl.when(jnp.logical_not(here))
            def _():
                pltpu.make_async_remote_copy(
                    source, back.at[zl, zh * 4 + x], s_back, r_back,
                    device_id=(target, y * 2 + h), device_id_type=MESH,
                ).start()

            @pl.when(here)
            def _():
                pltpu.make_async_copy(source, back.at[zl, zh * 4 + x], r_back).start()

    pltpu.make_async_copy(back, back, r_back).wait()

    def region(y_, zl_, k):
        rows = pl.ds(pl.multiple_of(16 * (y_ % 4), 16), 16)
        return out_ref.at[:, rows, pl.ds(pl.multiple_of(zl_ * 256 + k * 128, 128), 128)]

    def hand_on(piece, kind, k, target):
        pltpu.make_async_remote_copy(
            piece, piece, s_out, r_out.at[kind * 2 + k], device_id=target, device_id_type=MESH
        ).start()

    def arrived(piece, kind, k):
        pltpu.make_async_copy(piece, piece, r_out.at[kind * 2 + k]).wait()

    depths = pl.ds(pl.multiple_of(16 * y, 16), 16)
    for k in range(2):
        columns = pl.ds(pl.multiple_of(zl * 256 + k * 128, 128), 128)
        both = back[0, :, k] * back[1, :, k]
        out_ref[:, depths, columns] = jnp.transpose(both, (1, 0, 2)) * est_ref[:, depths, columns]
        own = region(y, zl, k)
        hand_on(own, 2, k, across)
        hand_on(own, 0, k, ahead)
        hand_on(own, 1, k, behind)

    arrived(region(y + 3, zl, 0), 0, 0)
    hand_on(region(y + 3, zl, 0), 3, 0, ahead)
    arrived(region(y + 1, zl, 1), 1, 1)
    hand_on(region(y + 1, zl, 1), 3, 1, behind)
    for k in range(2):
        arrived(region(y, over, k), 2, k)
        hand_on(region(y, over, k), 4, k, ahead)
        hand_on(region(y, over, k), 5, k, behind)
    for k in range(2):
        arrived(region(y + 2, zl, k), 3, k)
        hand_on(region(y + 2, zl, k), 6, k, across)
    arrived(region(y + 3, zl, 1), 0, 1)
    arrived(region(y + 1, zl, 0), 1, 0)
    for k in range(2):
        arrived(region(y + 3, over, k), 4, k)
        arrived(region(y + 1, over, k), 5, k)
        arrived(region(y + 2, over, k), 6, k)

    pltpu.make_async_copy(out_ref.at[0:7], out_ref.at[0:7], s_out).wait()
    pltpu.make_async_copy(est_t.at[0:15], est_t.at[0:15], s_est).wait()
    pltpu.make_async_copy(est_r.at[:, 8:136, :], est_r.at[:, 8:136, :], s_fwd).wait()
    pltpu.make_async_copy(cam_t, cam_t, s_cam).wait()

    @pl.when(core_of_y == c)
    def _():
        pltpu.make_async_copy(meta_s, meta_s, s_meta).wait()

    @pl.when(half_of_zh == c)
    def _():
        pltpu.make_async_copy(back.at[0, 0:15], back.at[0, 0:15], s_back).wait()
        pltpu.make_async_copy(back.at[1], back.at[1], s_back).wait()

    @pl.when(half_of_zh != c)
    def _():
        pltpu.make_async_copy(back, back, s_back).wait()


def shards(estimate, camera_blocks, block_lists, block_offsets, psf_index, psf_bank):
    bank = psf_bank[0].transpose(2, 0, 1)
    hbm = pl.BlockSpec(memory_space=pltpu.HBM)
    dma = pltpu.SemaphoreType.DMA
    return pl.pallas_call(
        kernel,
        out_shape=jax.ShapeDtypeStruct(estimate.shape, F32),
        in_specs=[hbm] * 5,
        out_specs=pl.BlockSpec(memory_space=pltpu.VMEM),
        scratch_shapes=[
            pltpu.VMEM(estimate.shape, F32),
            pltpu.VMEM(camera_blocks.shape, BF16),
            pltpu.VMEM(block_offsets.shape, jnp.int32),
            pltpu.SMEM(psf_index.shape, jnp.int32),
            pltpu.SMEM(bank.shape, F32),
            pltpu.VMEM((64, 16, 256), BF16),
            pltpu.VMEM((2, 32, 16, 256), BF16),
            pltpu.VMEM((16, GROUPS, 8, 128), F32),
            pltpu.VMEM((GROUPS, ROWS + 2 * PAD, 128), F32),
            pltpu.VMEM((4, META, 128), F32),
            pltpu.VMEM((2, META, 128), F32),
            pltpu.VMEM((2, 2, 16, 128), F32),
            pltpu.VMEM((2, 2 * TAPS, 8, 128), F32),
            pltpu.VMEM((2, GROUPS, ROWS, 1024), BF16),
            pltpu.VMEM((2, GROUPS, ROWS, 128), F32),
            pltpu.VMEM((2, GROUPS, ROWS + 2 * PAD, 128), F32),
            pltpu.VMEM((GROUPS, ROWS, 128), F32),
            pltpu.VMEM((GROUPS, 128, 128), F32),
            pltpu.VMEM((2, 16, 2, 8, 128), F32),
        ] + [dma((5,))] + [dma] * 13 + [dma((14,))],
        compiler_params=pltpu.CompilerParams(
            collective_id=0, has_side_effects=True, vmem_limit_bytes=56 * 1024 * 1024
        ),
        cost_estimate=pl.CostEstimate(flops=600_000_000, bytes_accessed=4_000_000, transcendentals=0),
    )(estimate, camera_blocks, block_offsets, psf_index, bank)


def solution(mesh):
    placed = (
        P("brick", None, None),
        P("view", "brick", None, None),
        P("view", None, None, None),
        P("view", None),
        P("view", None),
        P("view", None, None, None),
    )
    return jax.shard_map(
        shards, mesh=mesh, in_specs=placed, out_specs=P("brick", None, None), check_vma=False
    )
```

time: 70.6 us -> 67.5 us (0.956)
  the two profiles are of different devices: /device:TPU:1 before, /device:TPU:8 now
where the time goes in v2:
time: 67.5 us; the launch traced here: 67.4 us
  Pallas kernels  65.1 us (96%)
  local copies, waits for them, and re-layouts  2.26 us (3%)
    pallas_call x1, Pallas kernels, shards(): pl.pallas_call(kernel, out_shape=jax.ShapeDtypeStruct(estimate.shape, F32...  65.1 us
    unnamed x1, local copies, waits for them, and re-layouts  2.26 us

profile of v2, /device:TPU:8, one launch (start us, length us, event | category | flops | bytes accessed | tf_op | source)
XLA Modules:
  0.0 67.4 jit_solution(427309160856976349)
XLA Ops:
  0.0 65.1 %shard_map.55 = f32[8,64,512]{2,1,0:T(8,128)} custom-call(f32[8,64,512]{2,1,0:T(8,128)} %est_hbm.1, bf16[1,16,8,2048]{3,2,1,0:T(8,128)(2,1)} %cam_hbm.1, s32[1,512]{1,0:T(1,128)} %starts_hbm.1, s32[1,64]{1,0:T(1,128)} %index_hbm.1, f32[9,2,16]{2,1,0:T(2,128)} %bitcast.3), custom_call_target="tpu_custom_call" | custom-call | flops 600000000 | bytes 4000000 | tf_op jit(solution)/shard_map/pallas_call | solution.py:369
  65.1 2.3 %copy.7 = f32[8,64,512]{2,1,0:T(8,128)} copy(f32[8,64,512]{2,1,0:T(8,128)} %shard_map.55) | data formatting | bytes 2097152

commit v3 on v2

--- a/solution.py
+++ b/solution.py
@@ -16,6 +16,8 @@
 GROUPS = 4
 PAD = 8
 META = 24
+MIDDLE = 1.25
+STEPS = 43688.0
 
 
 def column_pass(parts, tap, reverse):
@@ -52,7 +54,7 @@
 def kernel(
     est_hbm, cam_hbm, starts_hbm, index_hbm, bank_hbm, out_ref,
     est_ref, cam_ref, starts_ref, index_ref, bank_ref,
-    cam_t, cam_r, est_t, est_r, meta_s, meta_r, table, taps, onehot, blurred, ratio, part, other, back,
+    cam_t, cam_r, est_t, est_q, est_r, meta_s, meta_r, table, taps, onehot, blurred, measured, ratio, part, other, back,
     s_load, s_est, r_est, s_fwd, r_fwd, s_meta, r_meta, s_cam, r_cam, s_half, r_half, s_back, r_back, s_out, r_out,
 ):
     brick = lax.axis_index("brick")
@@ -121,9 +123,14 @@
             ratio[w, g, 0:PAD, :] = jnp.zeros((PAD, 128), F32)
             ratio[w, g, PAD + ROWS:, :] = jnp.zeros((PAD, 128), F32)
     loads[0].wait()
-    for g in range(GROUPS):
-        cells = est_ref[:, pl.ds(pl.multiple_of(16 * y, 16), 16), g * 128:(g + 1) * 128]
-        est_t[:, g] = jnp.transpose(cells, (1, 0, 2))
+    for g in range(2):
+        halves = []
+        for h in range(2):
+            first = h * 256 + g * 128
+            cells = est_ref[:, pl.ds(pl.multiple_of(16 * y, 16), 16), first:first + 128]
+            halves.append(jnp.transpose(cells, (1, 0, 2)))
+        pair = jnp.round((jnp.concatenate(halves, axis=1) - MIDDLE) * STEPS)
+        est_t[:, :, g * 128:(g + 1) * 128] = pair.astype(jnp.int32).astype(jnp.int16)
     for load in loads[1:4]:
         load.wait()
     for k in range(4):
@@ -136,7 +143,7 @@
 
     back_same = (half_of_zh == c).astype(jnp.int32)
     pl.semaphore_wait(barrier, 64 + 15 + (32 - back_same) + 4)
-    own_rows = pl.ds(pl.multiple_of(PAD + 8 * brick, 8), 8)
+    slot_here = zh * 4 + x
 
     @pl.loop(0, 15)
     def _(n):
@@ -144,11 +151,11 @@
         zh_, zl_ = target_of(i // 4)
         x_ = (x + i % 4) % 4
         pltpu.make_async_remote_copy(
-            est_t.at[zh_ * 4 + x_], est_r.at[:, own_rows, :], s_est, r_est,
+            est_t.at[zh_ * 4 + x_], est_q.at[c, slot_here], s_est, r_est,
             device_id=place(zh_, x_, c, y, zl_), device_id_type=MESH,
         ).start()
 
-    pltpu.make_async_copy(est_t.at[zh * 4 + x], est_r.at[:, own_rows, :], r_est).start()
+    pltpu.make_async_copy(est_t.at[slot_here], est_q.at[c, slot_here], r_est).start()
 
     @pl.when(core_of_y == c)
     def _():
@@ -166,7 +173,8 @@
 
     @pl.loop(0, 16)
     def _(i):
-        y_, zh_ = (y + i // 4) % 4, (zh + i % 4) % 4
+        m = (i // 8) * 2 + i % 2
+        y_, zh_ = (y + (i // 2) % 4) % 4, (zh + 1 + zl + m) % 4
         quad = y_ * 4 + zh_
         start = pl.multiple_of(quad * 128, 128)
         for g in range(2):
@@ -187,46 +195,56 @@
             x_ = (x + n) % 4
             depth = quad * 4 + x_
             pltpu.make_async_remote_copy(
-                cam_t.at[depth], cam_r.at[y % 2, brick], s_cam, r_cam,
+                cam_t.at[depth], cam_r.at[y % 2, brick], s_cam, r_cam.at[m // 2],
                 device_id=place(zh_, x_, core_of_y, y_, over), device_id_type=MESH,
             ).start()
 
-    pltpu.make_async_copy(est_r.at[:, 8:136, :], est_r.at[:, 8:136, :], r_est).wait()
-
-    @pl.loop(0, 16)
-    def _(i):
-        rows = pl.ds(pl.multiple_of(PAD + 8 * (2 * i + c), 8), 8)
-        pltpu.make_async_remote_copy(
-            est_r.at[:, rows, :], est_r.at[:, rows, :], s_fwd, r_fwd,
-            device_id=partner, device_id_type=MESH,
-        ).start()
+    pltpu.make_async_copy(est_q.at[c], est_q.at[c], r_est).wait()
+    pltpu.make_async_remote_copy(
+        est_q.at[c], est_q.at[c], s_fwd, r_fwd, device_id=partner, device_id_type=MESH
+    ).start()
 
     pltpu.make_async_copy(meta_r, meta_r, r_meta).wait()
     row_id = lax.broadcasted_iota(jnp.int32, (ROWS, 128), 0).astype(F32)
+    row = lax.broadcasted_iota(jnp.int32, (16, 512), 0)
     block = lax.broadcasted_iota(jnp.int32, (16, 512), 1)
-    tile = lax.broadcasted_iota(jnp.int32, (16, 512), 0)
-    holder = lax.broadcasted_iota(jnp.int32, (512, 256), 0) // 16
-    owner = lax.broadcasted_iota(jnp.int32, (512, 256), 1) // 8
-    spread = jnp.where(holder == owner, 1.0, 0.0).astype(BF16)
+    chosen = (block // 128 == row // 4) & ((block % 16) // 4 == row % 4)
+    block_ = lax.broadcasted_iota(jnp.int32, (512, 256), 0)
+    entry = lax.broadcasted_iota(jnp.int32, (512, 256), 1)
+    spread = ((block_ // 16) % 8 == (entry % 64) // 8) & (block_ % 4 == entry // 64)
+    spread = jnp.where(spread, 1.0, 0.0).astype(BF16)
     inside = (lax.broadcasted_iota(jnp.int32, (16, 256), 1) % 8).astype(F32)
+
+    def plane(m):
+        return (zh + zl + 6 - m) % 4
+
     for w in range(2):
         for q in range(2 * TAPS):
             taps[w, q] = jnp.broadcast_to(meta_r[w, q:q + 1, :], (8, 128))
         starts = jnp.concatenate([meta_r[w, 20 + n:21 + n, :] for n in range(4)], axis=1)
-        by_tile = jnp.where(block % 16 == tile, jnp.broadcast_to(starts, (16, 512)), 0.0).astype(BF16)
+        by_tile = jnp.where(chosen, jnp.broadcast_to(starts, (16, 512)), 0.0).astype(BF16)
         rows_of = jnp.dot(by_tile, spread, preferred_element_type=F32) + inside
         for k in range(2):
             table[w, k] = rows_of[:, k * 128:(k + 1) * 128]
 
         @pl.loop(0, GROUPS)
         def _(g):
-            for n in range(4):
+            for m in range(4):
                 for k in range(2):
-                    first = table[w, k, pl.ds(g * 4 + n, 1), :]
+                    first = table[w, k, pl.ds(plane(m) * 4 + g, 1), :]
                     hit = jnp.where(row_id == first, 1.0, 0.0).astype(BF16)
-                    onehot[w, g, :, n * 256 + k * 128:n * 256 + (k + 1) * 128] = hit
-
-    pltpu.make_async_copy(est_r.at[:, 8:136, :], est_r.at[:, 8:136, :], r_fwd).wait()
+                    lanes = (m % 2) * 256 + k * 128
+                    onehot[w, m // 2, g, :, lanes:lanes + 128] = hit
+
+    pltpu.make_async_copy(est_q.at[1 - c], est_q.at[1 - c], r_fwd).wait()
+
+    @pl.loop(0, 32)
+    def _(d):
+        cells = est_q[d % 2, d // 2].astype(jnp.int32).astype(F32) * (1.0 / STEPS) + MIDDLE
+        rows = pl.ds(pl.multiple_of(PAD + 8 * d, 8), 8)
+        for g in range(GROUPS):
+            h, lanes = g // 2, (g % 2) * 128
+            est_r[g, rows, :] = cells[h * 8:(h + 1) * 8, lanes:lanes + 128]
 
     @pl.loop(0, ROWS // 8)
     def _(i):
@@ -240,20 +258,27 @@
             for g in range(GROUPS):
                 blurred[w, g, pl.ds(row, 8), :] = sums[g]
 
-    pltpu.make_async_copy(cam_r, cam_r, r_cam).wait()
-    block_lane = lax.broadcasted_iota(jnp.int32, (ROWS, 128), 1) // 32
-
-    @pl.loop(0, 2)
-    def _(w):
-        for g in range(GROUPS):
-            h = g // 2
-            cells = cam_r[w, :, :, (g % 2) * 128:(g % 2 + 1) * 128].astype(F32)
-            cells = cells[:, h * 8:(h + 1) * 8, :].reshape(ROWS, 128)
-            stack = jnp.concatenate(
-                [jnp.where(block_lane == n, cells, 0.0).astype(BF16) for n in range(4)], axis=0
-            )
-            measured = jnp.dot(onehot[w, g], stack, preferred_element_type=F32)
-            ratio[w, g, PAD:PAD + ROWS, :] = measured / blurred[w, g]
+    block_lane = lax.broadcasted_iota(jnp.int32, (64, 128), 1) // 32
+    for half in range(2):
+        pltpu.make_async_copy(cam_r.at[half], cam_r.at[half], r_cam.at[half]).wait()
+
+        @pl.loop(0, 2)
+        def _(w):
+            for g in range(GROUPS):
+                h = g // 2
+                stack = []
+                for m in (2 * half, 2 * half + 1):
+                    holders = pl.ds(pl.multiple_of(plane(m) * 8, 8), 8)
+                    cells = cam_r[w, holders, :, (g % 2) * 128:(g % 2 + 1) * 128].astype(F32)
+                    cells = cells[:, h * 8:(h + 1) * 8, :].reshape(64, 128)
+                    stack += [jnp.where(block_lane == n, cells, 0.0).astype(BF16) for n in range(4)]
+                landed = jnp.dot(
+                    onehot[w, half, g], jnp.concatenate(stack, axis=0), preferred_element_type=F32
+                )
+                if half == 0:
+                    measured[w, g] = landed
+                else:
+                    ratio[w, g, PAD:PAD + ROWS, :] = (measured[w, g] + landed) / blurred[w, g]
 
     def correct(first):
         @pl.loop(0, 16)
@@ -272,36 +297,35 @@
 
     correct((1 - c) * 128)
     theirs = part.at[:, pl.ds(pl.multiple_of((1 - c) * 128, 128), 128), :]
-    half = pltpu.make_async_remote_copy(
+    swap = pltpu.make_async_remote_copy(
         theirs, other, s_half, r_half, device_id=partner, device_id_type=MESH
     )
-    half.start()
+    swap.start()
     correct(c * 128)
-    half.wait()
-
-    @pl.loop(0, 16)
-    def _(i):
-        slot = (brick + i) % 16
-        target = 16 * c + slot
-        rows = pl.ds(pl.multiple_of(8 * slot, 8), 8)
-        here_rows = pl.ds(pl.multiple_of(c * 128 + 8 * slot, 8), 8)
-        other[:, rows, :] = other[:, rows, :] * part[:, here_rows, :]
-        for h in range(2):
-            here = (target == brick) & (h == zl)
-            source = other.at[2 * h:2 * h + 2, rows, :]
-
-            @pl.when(jnp.logical_not(here))
-            def _():
-                pltpu.make_async_remote_copy(
-                    source, back.at[zl, zh * 4 + x], s_back, r_back,
-                    device_id=(target, y * 2 + h), device_id_type=MESH,
-                ).start()
-
-            @pl.when(here)
-            def _():
-                pltpu.make_async_copy(source, back.at[zl, zh * 4 + x], r_back).start()
-
-    pltpu.make_async_copy(back, back, r_back).wait()
+    swap.wait()
+
+    for k in range(2):
+        @pl.loop(0, 16)
+        def _(i):
+            slot = (brick + i) % 16
+            target = 16 * c + slot
+            rows = pl.ds(pl.multiple_of(8 * slot, 8), 8)
+            here_rows = pl.ds(pl.multiple_of(c * 128 + 8 * slot, 8), 8)
+            for h in range(2):
+                here = (target == brick) & (h == zl)
+                other[2 * h + k, rows, :] = other[2 * h + k, rows, :] * part[2 * h + k, here_rows, :]
+                source, landing = other.at[2 * h + k, rows, :], back.at[k, zl, slot_here]
+
+                @pl.when(jnp.logical_not(here))
+                def _():
+                    pltpu.make_async_remote_copy(
+                        source, landing, s_back, r_back.at[k],
+                        device_id=(target, y * 2 + h), device_id_type=MESH,
+                    ).start()
+
+                @pl.when(here)
+                def _():
+                    pltpu.make_async_copy(source, landing, r_back.at[k]).start()
 
     def region(y_, zl_, k):
         rows = pl.ds(pl.multiple_of(16 * (y_ % 4), 16), 16)
@@ -318,7 +342,8 @@
     depths = pl.ds(pl.multiple_of(16 * y, 16), 16)
     for k in range(2):
         columns = pl.ds(pl.multiple_of(zl * 256 + k * 128, 128), 128)
-        both = back[0, :, k] * back[1, :, k]
+        pltpu.make_async_copy(back.at[k], back.at[k], r_back.at[k]).wait()
+        both = back[k, 0] * back[k, 1]
         out_ref[:, depths, columns] = jnp.transpose(both, (1, 0, 2)) * est_ref[:, depths, columns]
         own = region(y, zl, k)
         hand_on(own, 2, k, across)
@@ -345,7 +370,7 @@
 
     pltpu.make_async_copy(out_ref.at[0:7], out_ref.at[0:7], s_out).wait()
     pltpu.make_async_copy(est_t.at[0:15], est_t.at[0:15], s_est).wait()
-    pltpu.make_async_copy(est_r.at[:, 8:136, :], est_r.at[:, 8:136, :], s_fwd).wait()
+    pltpu.make_async_copy(est_q.at[c], est_q.at[c], s_fwd).wait()
     pltpu.make_async_copy(cam_t, cam_t, s_cam).wait()
 
     @pl.when(core_of_y == c)
@@ -354,8 +379,9 @@
 
     @pl.when(half_of_zh == c)
     def _():
-        pltpu.make_async_copy(back.at[0, 0:15], back.at[0, 0:15], s_back).wait()
-        pltpu.make_async_copy(back.at[1], back.at[1], s_back).wait()
+        pltpu.make_async_copy(back.at[0], back.at[0], s_back).wait()
+        pltpu.make_async_copy(back.at[1, 0], back.at[1, 0], s_back).wait()
+        pltpu.make_async_copy(back.at[1, 1, 0:14], back.at[1, 1, 0:14], s_back).wait()
 
     @pl.when(half_of_zh != c)
     def _():
@@ -379,24 +405,26 @@
             pltpu.SMEM(bank.shape, F32),
             pltpu.VMEM((64, 16, 256), BF16),
             pltpu.VMEM((2, 32, 16, 256), BF16),
-            pltpu.VMEM((16, GROUPS, 8, 128), F32),
+            pltpu.VMEM((16, 16, 256), jnp.int16),
+            pltpu.VMEM((2, 16, 16, 256), jnp.int16),
             pltpu.VMEM((GROUPS, ROWS + 2 * PAD, 128), F32),
             pltpu.VMEM((4, META, 128), F32),
             pltpu.VMEM((2, META, 128), F32),
             pltpu.VMEM((2, 2, 16, 128), F32),
             pltpu.VMEM((2, 2 * TAPS, 8, 128), F32),
-            pltpu.VMEM((2, GROUPS, ROWS, 1024), BF16),
+            pltpu.VMEM((2, 2, GROUPS, ROWS, 512), BF16),
+            pltpu.VMEM((2, GROUPS, ROWS, 128), F32),
             pltpu.VMEM((2, GROUPS, ROWS, 128), F32),
             pltpu.VMEM((2, GROUPS, ROWS + 2 * PAD, 128), F32),
             pltpu.VMEM((GROUPS, ROWS, 128), F32),
             pltpu.VMEM((GROUPS, 128, 128), F32),
-            pltpu.VMEM((2, 16, 2, 8, 128), F32),
-        ] + [dma((5,))] + [dma] * 13 + [dma((14,))],
+            pltpu.VMEM((2, 2, 16, 8, 128), F32),
+        ] + [dma((5,))] + [dma] * 7 + [dma((2,))] + [dma] * 3 + [dma((2,)), dma, dma((14,))],
         compiler_params=pltpu.CompilerParams(
-            collective_id=0, has_side_effects=True, vmem_limit_bytes=56 * 1024 * 1024
+            collective_id=0, has_side_effects=True, vmem_limit_bytes=40 * 1024 * 1024
         ),
         cost_estimate=pl.CostEstimate(flops=600_000_000, bytes_accessed=4_000_000, transcendentals=0),
-    )(estimate, camera_blocks, block_offsets, psf_index, bank)
+    )(*[pltpu.with_memory_space_constraint(a, pltpu.HBM) for a in (estimate, camera_blocks, block_offsets, psf_index, bank)])
 
 
 def solution(mesh):

time: 67.5 us -> 60.3 us (0.89)
  Pallas kernels: 65.1 us -> 59.3 us
  local copies, waits for them, and re-layouts: 2.26 us -> 0.97 us
    pallas_call x1, Pallas kernels: 65.1 us -> 59.3 us  [shards(): pl.pallas_call(kernel, out_shape=jax.ShapeDtypeStruct(estimate.shape, F32...]
    unnamed x1, local copies, waits for them, and re-layouts: 2.26 us -> 0.97 us
where the time goes in v3:
time: 60.3 us
  Pallas kernels  59.3 us (98%)
  local copies, waits for them, and re-layouts  0.97 us (2%)
    pallas_call x1, Pallas kernels, shards(): pl.pallas_call(kernel, out_shape=jax.ShapeDtypeStruct(estimate.shape, F32...  59.3 us

profile of v3, /device:TPU:8, one launch (start us, length us, event | category | flops | bytes accessed | tf_op | source)
XLA Modules:
  0.0 60.3 jit_solution(16813441972988255705)
XLA Ops:
  0.0 59.3 %shard_map.55 = f32[8,64,512]{2,1,0:T(8,128)S(1)} custom-call(f32[8,64,512]{2,1,0:T(8,128)} %est_hbm.1, bf16[1,16,8,2048]{3,2,1,0:T(8,128)(2,1)} %cam_hbm.1, s32[1,512]{1,0:T(1,128)} %starts_hbm.1, s32[1,64]{1,0:T(1,128)} %index_hbm.1, f32[9,2,16]{2,1,0:T(2,128)} %bitcast.3), custom_call_target="tpu_custom_call" | custom-call | flops 600000000 | bytes 4000000 | tf_op jit(solution)/shard_map/pallas_call | solution.py:395
  59.3 1.0 %copy.7 = f32[8,64,512]{2,1,0:T(8,128)} copy(f32[8,64,512]{2,1,0:T(8,128)S(1)} %shard_map.55) | data formatting | bytes 2097152

commit v4 on v3

--- a/solution.py
+++ b/solution.py
@@ -54,7 +54,7 @@
 def kernel(
     est_hbm, cam_hbm, starts_hbm, index_hbm, bank_hbm, out_ref,
     est_ref, cam_ref, starts_ref, index_ref, bank_ref,
-    cam_t, cam_r, est_t, est_q, est_r, meta_s, meta_r, table, taps, onehot, blurred, measured, ratio, part, other, back,
+    cam_t, cam_r, est_t, est_q, est_r, meta_s, meta_r, table, taps, onehot, blurred, ratio, part, other, back,
     s_load, s_est, r_est, s_fwd, r_fwd, s_meta, r_meta, s_cam, r_cam, s_half, r_half, s_back, r_back, s_out, r_out,
 ):
     brick = lax.axis_index("brick")
@@ -173,8 +173,7 @@
 
     @pl.loop(0, 16)
     def _(i):
-        m = (i // 8) * 2 + i % 2
-        y_, zh_ = (y + (i // 2) % 4) % 4, (zh + 1 + zl + m) % 4
+        y_, zh_ = (y + i // 4) % 4, (zh + i % 4) % 4
         quad = y_ * 4 + zh_
         start = pl.multiple_of(quad * 128, 128)
         for g in range(2):
@@ -195,7 +194,7 @@
             x_ = (x + n) % 4
             depth = quad * 4 + x_
             pltpu.make_async_remote_copy(
-                cam_t.at[depth], cam_r.at[y % 2, brick], s_cam, r_cam.at[m // 2],
+                cam_t.at[depth], cam_r.at[y % 2, brick], s_cam, r_cam.at[y % 2],
                 device_id=place(zh_, x_, core_of_y, y_, over), device_id_type=MESH,
             ).start()
 
@@ -215,9 +214,6 @@
     spread = jnp.where(spread, 1.0, 0.0).astype(BF16)
     inside = (lax.broadcasted_iota(jnp.int32, (16, 256), 1) % 8).astype(F32)
 
-    def plane(m):
-        return (zh + zl + 6 - m) % 4
-
     for w in range(2):
         for q in range(2 * TAPS):
             taps[w, q] = jnp.broadcast_to(meta_r[w, q:q + 1, :], (8, 128))
@@ -231,10 +227,9 @@
         def _(g):
             for m in range(4):
                 for k in range(2):
-                    first = table[w, k, pl.ds(plane(m) * 4 + g, 1), :]
+                    first = table[w, k, pl.ds(m * 4 + g, 1), :]
                     hit = jnp.where(row_id == first, 1.0, 0.0).astype(BF16)
-                    lanes = (m % 2) * 256 + k * 128
-                    onehot[w, m // 2, g, :, lanes:lanes + 128] = hit
+                    onehot[w, g, :, m * 256 + k * 128:m * 256 + (k + 1) * 128] = hit
 
     pltpu.make_async_copy(est_q.at[1 - c], est_q.at[1 - c], r_fwd).wait()
 
@@ -246,62 +241,59 @@
             h, lanes = g // 2, (g % 2) * 128
             est_r[g, rows, :] = cells[h * 8:(h + 1) * 8, lanes:lanes + 128]
 
-    @pl.loop(0, ROWS // 8)
+    @pl.loop(0, ROWS // 16)
     def _(i):
-        row = pl.multiple_of(8 * i, 8)
-        for w in range(2):
-            parts = [
-                row_pass(lambda s, g=g: est_r[g, pl.ds(row + (PAD + s), 8), :], lambda q: taps[w, q], False)
-                for g in range(GROUPS)
-            ]
-            sums = column_pass(parts, lambda q: taps[w, TAPS + q], False)
-            for g in range(GROUPS):
-                blurred[w, g, pl.ds(row, 8), :] = sums[g]
+        for n in range(2):
+            row = pl.multiple_of(16 * i + 8 * n, 8)
+            for w in range(2):
+                parts = [
+                    row_pass(lambda s, g=g: est_r[g, pl.ds(row + (PAD + s), 8), :], lambda q: taps[w, q], False)
+                    for g in range(GROUPS)
+                ]
+                sums = column_pass(parts, lambda q: taps[w, TAPS + q], False)
+                for g in range(GROUPS):
+                    blurred[w, g, pl.ds(row, 8), :] = sums[g]
 
     block_lane = lax.broadcasted_iota(jnp.int32, (64, 128), 1) // 32
-    for half in range(2):
-        pltpu.make_async_copy(cam_r.at[half], cam_r.at[half], r_cam.at[half]).wait()
-
-        @pl.loop(0, 2)
-        def _(w):
-            for g in range(GROUPS):
-                h = g // 2
-                stack = []
-                for m in (2 * half, 2 * half + 1):
-                    holders = pl.ds(pl.multiple_of(plane(m) * 8, 8), 8)
-                    cells = cam_r[w, holders, :, (g % 2) * 128:(g % 2 + 1) * 128].astype(F32)
-                    cells = cells[:, h * 8:(h + 1) * 8, :].reshape(64, 128)
-                    stack += [jnp.where(block_lane == n, cells, 0.0).astype(BF16) for n in range(4)]
-                landed = jnp.dot(
-                    onehot[w, half, g], jnp.concatenate(stack, axis=0), preferred_element_type=F32
-                )
-                if half == 0:
-                    measured[w, g] = landed
-                else:
-                    ratio[w, g, PAD:PAD + ROWS, :] = (measured[w, g] + landed) / blurred[w, g]
-
-    def correct(first):
-        @pl.loop(0, 16)
+
+    def measure(w):
+        pltpu.make_async_copy(cam_r.at[w], cam_r.at[w], r_cam.at[w]).wait()
+        for g in range(GROUPS):
+            h = g // 2
+            stack = []
+            for m in range(4):
+                cells = cam_r[w, m * 8:(m + 1) * 8, :, (g % 2) * 128:(g % 2 + 1) * 128].astype(F32)
+                cells = cells[:, h * 8:(h + 1) * 8, :].reshape(64, 128)
+                stack += [jnp.where(block_lane == n, cells, 0.0).astype(BF16) for n in range(4)]
+            measured = jnp.dot(onehot[w, g], jnp.concatenate(stack, axis=0), preferred_element_type=F32)
+            ratio[w, g, PAD:PAD + ROWS, :] = measured / blurred[w, g]
+
+    def correct(w, first, rows, join):
+        @pl.loop(0, rows // 16)
         def _(i):
-            row = pl.multiple_of(first + 8 * i, 8)
-            product = None
-            for w in range(2):
+            for n in range(2):
+                row = pl.multiple_of(first + 16 * i + 8 * n, 8)
                 parts = [
                     row_pass(lambda s, g=g: ratio[w, g, pl.ds(row + (PAD + s), 8), :], lambda q: taps[w, q], True)
                     for g in range(GROUPS)
                 ]
                 sums = column_pass(parts, lambda q: taps[w, TAPS + q], True)
-                product = sums if product is None else [a * b for a, b in zip(product, sums)]
-            for g in range(GROUPS):
-                part[g, pl.ds(row, 8), :] = product[g]
-
-    correct((1 - c) * 128)
+                for g in range(GROUPS):
+                    so_far = part[g, pl.ds(row, 8), :] * sums[g] if join else sums[g]
+                    part[g, pl.ds(row, 8), :] = so_far
+
+    early = jnp.where((y - 2 * c + 4) % 4 == 0, 0, 1)
+    measure(early)
+    correct(early, 0, ROWS, False)
+    late = 1 - early
+    measure(late)
+    correct(late, (1 - c) * 128, 128, True)
     theirs = part.at[:, pl.ds(pl.multiple_of((1 - c) * 128, 128), 128), :]
     swap = pltpu.make_async_remote_copy(
         theirs, other, s_half, r_half, device_id=partner, device_id_type=MESH
     )
     swap.start()
-    correct(c * 128)
+    correct(late, c * 128, 128, True)
     swap.wait()
 
     for k in range(2):
@@ -340,27 +332,36 @@
         pltpu.make_async_copy(piece, piece, r_out.at[kind * 2 + k]).wait()
 
     depths = pl.ds(pl.multiple_of(16 * y, 16), 16)
-    for k in range(2):
+
+    def begin(k):
+        pltpu.make_async_copy(back.at[k], back.at[k], r_back.at[k]).wait()
         columns = pl.ds(pl.multiple_of(zl * 256 + k * 128, 128), 128)
-        pltpu.make_async_copy(back.at[k], back.at[k], r_back.at[k]).wait()
         both = back[k, 0] * back[k, 1]
         out_ref[:, depths, columns] = jnp.transpose(both, (1, 0, 2)) * est_ref[:, depths, columns]
         own = region(y, zl, k)
         hand_on(own, 2, k, across)
-        hand_on(own, 0, k, ahead)
-        hand_on(own, 1, k, behind)
-
-    arrived(region(y + 3, zl, 0), 0, 0)
-    hand_on(region(y + 3, zl, 0), 3, 0, ahead)
-    arrived(region(y + 1, zl, 1), 1, 1)
-    hand_on(region(y + 1, zl, 1), 3, 1, behind)
-    for k in range(2):
+        hand_on(own, k, k, behind if k else ahead)
+        hand_on(own, 1 - k, k, ahead if k else behind)
+
+    def sideways(k):
         arrived(region(y, over, k), 2, k)
         hand_on(region(y, over, k), 4, k, ahead)
         hand_on(region(y, over, k), 5, k, behind)
-    for k in range(2):
+
+    def far(k):
         arrived(region(y + 2, zl, k), 3, k)
         hand_on(region(y + 2, zl, k), 6, k, across)
+
+    begin(0)
+    arrived(region(y + 3, zl, 0), 0, 0)
+    hand_on(region(y + 3, zl, 0), 3, 0, ahead)
+    sideways(0)
+    begin(1)
+    far(0)
+    arrived(region(y + 1, zl, 1), 1, 1)
+    hand_on(region(y + 1, zl, 1), 3, 1, behind)
+    sideways(1)
+    far(1)
     arrived(region(y + 3, zl, 1), 0, 1)
     arrived(region(y + 1, zl, 0), 1, 0)
     for k in range(2):
@@ -412,8 +413,7 @@
             pltpu.VMEM((2, META, 128), F32),
             pltpu.VMEM((2, 2, 16, 128), F32),
             pltpu.VMEM((2, 2 * TAPS, 8, 128), F32),
-            pltpu.VMEM((2, 2, GROUPS, ROWS, 512), BF16),
-            pltpu.VMEM((2, GROUPS, ROWS, 128), F32),
+            pltpu.VMEM((2, GROUPS, ROWS, 1024), BF16),
             pltpu.VMEM((2, GROUPS, ROWS, 128), F32),
             pltpu.VMEM((2, GROUPS, ROWS + 2 * PAD, 128), F32),
             pltpu.VMEM((GROUPS, ROWS, 128), F32),

time: 60.3 us -> 63.2 us (1.048)
  the two profiles are of different devices: /device:TPU:8 before, /device:TPU:16 now
where the time goes in v4:
time: 63.2 us
  Pallas kernels  62.2 us (98%)
  local copies, waits for them, and re-layouts  0.97 us (2%)
    pallas_call x1, Pallas kernels, shards(): pl.pallas_call(kernel, out_shape=jax.ShapeDtypeStruct(estimate.shape, F32...  62.2 us

profile of v4, /device:TPU:16, one launch (start us, length us, event | category | flops | bytes accessed | tf_op | source)
XLA Modules:
  0.0 63.2 jit_solution(8384814647603606368)
XLA Ops:
  0.0 62.2 %shard_map.55 = f32[8,64,512]{2,1,0:T(8,128)S(1)} custom-call(f32[8,64,512]{2,1,0:T(8,128)} %est_hbm.1, bf16[1,16,8,2048]{3,2,1,0:T(8,128)(2,1)} %cam_hbm.1, s32[1,512]{1,0:T(1,128)} %starts_hbm.1, s32[1,64]{1,0:T(1,128)} %index_hbm.1, f32[9,2,16]{2,1,0:T(2,128)} %bitcast.3), custom_call_target="tpu_custom_call" | custom-call | flops 600000000 | bytes 4000000 | tf_op jit(solution)/shard_map/pallas_call | solution.py:396
  62.2 1.0 %copy.7 = f32[8,64,512]{2,1,0:T(8,128)} copy(f32[8,64,512]{2,1,0:T(8,128)S(1)} %shard_map.55) | data formatting | bytes 2097152

commit v5 on v4

--- a/solution.py
+++ b/solution.py
@@ -269,10 +269,10 @@
             ratio[w, g, PAD:PAD + ROWS, :] = measured / blurred[w, g]
 
     def correct(w, first, rows, join):
-        @pl.loop(0, rows // 16)
+        @pl.loop(0, rows // 32)
         def _(i):
-            for n in range(2):
-                row = pl.multiple_of(first + 16 * i + 8 * n, 8)
+            for n in range(4):
+                row = pl.multiple_of(first + 32 * i + 8 * n, 8)
                 parts = [
                     row_pass(lambda s, g=g: ratio[w, g, pl.ds(row + (PAD + s), 8), :], lambda q: taps[w, q], True)
                     for g in range(GROUPS)
@@ -319,55 +319,50 @@
                 def _():
                     pltpu.make_async_copy(source, landing, r_back.at[k]).start()
 
-    def region(y_, zl_, k):
-        rows = pl.ds(pl.multiple_of(16 * (y_ % 4), 16), 16)
-        return out_ref.at[:, rows, pl.ds(pl.multiple_of(zl_ * 256 + k * 128, 128), 128)]
-
-    def hand_on(piece, kind, k, target):
+    def region(y_, zl_, q):
+        rows = pl.ds(pl.multiple_of(16 * (y_ % 4) + 8 * (q % 2), 8), 8)
+        return out_ref.at[:, rows, pl.ds(pl.multiple_of(zl_ * 256 + q // 2 * 128, 128), 128)]
+
+    def hand_on(piece, kind, q, target):
         pltpu.make_async_remote_copy(
-            piece, piece, s_out, r_out.at[kind * 2 + k], device_id=target, device_id_type=MESH
+            piece, piece, s_out, r_out.at[kind * 4 + q], device_id=target, device_id_type=MESH
         ).start()
 
-    def arrived(piece, kind, k):
-        pltpu.make_async_copy(piece, piece, r_out.at[kind * 2 + k]).wait()
-
-    depths = pl.ds(pl.multiple_of(16 * y, 16), 16)
-
-    def begin(k):
+    def arrived(piece, kind, q):
+        pltpu.make_async_copy(piece, piece, r_out.at[kind * 4 + q]).wait()
+
+    for k in range(2):
         pltpu.make_async_copy(back.at[k], back.at[k], r_back.at[k]).wait()
         columns = pl.ds(pl.multiple_of(zl * 256 + k * 128, 128), 128)
-        both = back[k, 0] * back[k, 1]
-        out_ref[:, depths, columns] = jnp.transpose(both, (1, 0, 2)) * est_ref[:, depths, columns]
-        own = region(y, zl, k)
-        hand_on(own, 2, k, across)
-        hand_on(own, k, k, behind if k else ahead)
-        hand_on(own, 1 - k, k, ahead if k else behind)
-
-    def sideways(k):
-        arrived(region(y, over, k), 2, k)
-        hand_on(region(y, over, k), 4, k, ahead)
-        hand_on(region(y, over, k), 5, k, behind)
-
-    def far(k):
-        arrived(region(y + 2, zl, k), 3, k)
-        hand_on(region(y + 2, zl, k), 6, k, across)
-
-    begin(0)
-    arrived(region(y + 3, zl, 0), 0, 0)
-    hand_on(region(y + 3, zl, 0), 3, 0, ahead)
-    sideways(0)
-    begin(1)
-    far(0)
-    arrived(region(y + 1, zl, 1), 1, 1)
-    hand_on(region(y + 1, zl, 1), 3, 1, behind)
-    sideways(1)
-    far(1)
-    arrived(region(y + 3, zl, 1), 0, 1)
-    arrived(region(y + 1, zl, 0), 1, 0)
-    for k in range(2):
-        arrived(region(y + 3, over, k), 4, k)
-        arrived(region(y + 1, over, k), 5, k)
-        arrived(region(y + 2, over, k), 6, k)
+        for d in range(2):
+            q = 2 * k + d
+            depths = pl.ds(pl.multiple_of(16 * y + 8 * d, 8), 8)
+            both = back[k, 0, 8 * d:8 * d + 8] * back[k, 1, 8 * d:8 * d + 8]
+            out_ref[:, depths, columns] = jnp.transpose(both, (1, 0, 2)) * est_ref[:, depths, columns]
+            own = region(y, zl, q)
+            hand_on(own, 0, q, ahead)
+            hand_on(own, 1, q, behind)
+            hand_on(own, 2, q, across)
+
+    for n in range(2):
+        arrived(region(y + 3, zl, n), 0, n)
+        hand_on(region(y + 3, zl, n), 3, n, ahead)
+        arrived(region(y + 1, zl, 2 + n), 1, 2 + n)
+        hand_on(region(y + 1, zl, 2 + n), 3, 2 + n, behind)
+    for q in range(4):
+        arrived(region(y, over, q), 2, q)
+        hand_on(region(y, over, q), 4, q, ahead)
+        hand_on(region(y, over, q), 5, q, behind)
+    for q in (0, 2, 1, 3):
+        arrived(region(y + 2, zl, q), 3, q)
+        hand_on(region(y + 2, zl, q), 6, q, across)
+    for n in range(2):
+        arrived(region(y + 3, zl, 2 + n), 0, 2 + n)
+        arrived(region(y + 1, zl, n), 1, n)
+    for q in range(4):
+        arrived(region(y + 3, over, q), 4, q)
+        arrived(region(y + 1, over, q), 5, q)
+        arrived(region(y + 2, over, q), 6, q)
 
     pltpu.make_async_copy(out_ref.at[0:7], out_ref.at[0:7], s_out).wait()
     pltpu.make_async_copy(est_t.at[0:15], est_t.at[0:15], s_est).wait()
@@ -419,7 +414,7 @@
             pltpu.VMEM((GROUPS, ROWS, 128), F32),
             pltpu.VMEM((GROUPS, 128, 128), F32),
             pltpu.VMEM((2, 2, 16, 8, 128), F32),
-        ] + [dma((5,))] + [dma] * 7 + [dma((2,))] + [dma] * 3 + [dma((2,)), dma, dma((14,))],
+        ] + [dma((5,))] + [dma] * 7 + [dma((2,))] + [dma] * 3 + [dma((2,)), dma, dma((28,))],
         compiler_params=pltpu.CompilerParams(
             collective_id=0, has_side_effects=True, vmem_limit_bytes=40 * 1024 * 1024
         ),

time: 63.2 us -> 57.7 us (0.913)
  the two profiles are of different devices: /device:TPU:16 before, /device:TPU:8 now
where the time goes in v5:
time: 57.7 us
  Pallas kernels  56.7 us (98%)
  local copies, waits for them, and re-layouts  0.97 us (2%)
    pallas_call x1, Pallas kernels, shards(): pl.pallas_call(kernel, out_shape=jax.ShapeDtypeStruct(estimate.shape, F32...  56.7 us

profile of v5, /device:TPU:8, one launch (start us, length us, event | category | flops | bytes accessed | tf_op | source)
XLA Modules:
  0.0 57.7 jit_solution(2770966573521839744)
XLA Ops:
  0.0 56.7 %shard_map.55 = f32[8,64,512]{2,1,0:T(8,128)S(1)} custom-call(f32[8,64,512]{2,1,0:T(8,128)} %est_hbm.1, bf16[1,16,8,2048]{3,2,1,0:T(8,128)(2,1)} %cam_hbm.1, s32[1,512]{1,0:T(1,128)} %starts_hbm.1, s32[1,64]{1,0:T(1,128)} %index_hbm.1, f32[9,2,16]{2,1,0:T(2,128)} %bitcast.3), custom_call_target="tpu_custom_call" | custom-call | flops 600000000 | bytes 4000000 | tf_op jit(solution)/shard_map/pallas_call | solution.py:391
  56.7 1.0 %copy.7 = f32[8,64,512]{2,1,0:T(8,128)} copy(f32[8,64,512]{2,1,0:T(8,128)S(1)} %shard_map.55) | data formatting | bytes 2097152

commit v6 on v5

--- a/solution.py
+++ b/solution.py
@@ -269,10 +269,10 @@
             ratio[w, g, PAD:PAD + ROWS, :] = measured / blurred[w, g]
 
     def correct(w, first, rows, join):
-        @pl.loop(0, rows // 32)
+        @pl.loop(0, rows // 64)
         def _(i):
-            for n in range(4):
-                row = pl.multiple_of(first + 32 * i + 8 * n, 8)
+            for n in range(8):
+                row = pl.multiple_of(first + 64 * i + 8 * n, 8)
                 parts = [
                     row_pass(lambda s, g=g: ratio[w, g, pl.ds(row + (PAD + s), 8), :], lambda q: taps[w, q], True)
                     for g in range(GROUPS)

time: 57.7 us -> 57.1 us (0.990)
  Pallas kernels: 56.7 us -> 56 us
    pallas_call x1, Pallas kernels: 56.7 us -> 56 us  [shards(): pl.pallas_call(kernel, out_shape=jax.ShapeDtypeStruct(estimate.shape, F32...]
where the time goes in v6:
time: 57.1 us; the launch traced here: 57 us
  Pallas kernels  56 us (98%)
  local copies, waits for them, and re-layouts  0.97 us (2%)
    pallas_call x1, Pallas kernels, shards(): pl.pallas_call(kernel, out_shape=jax.ShapeDtypeStruct(estimate.shape, F32...  56 us

profile of v6, /device:TPU:8, one launch (start us, length us, event | category | flops | bytes accessed | tf_op | source)
XLA Modules:
  0.0 57.0 jit_solution(17031291334847159562)
XLA Ops:
  0.0 56.0 %shard_map.55 = f32[8,64,512]{2,1,0:T(8,128)S(1)} custom-call(f32[8,64,512]{2,1,0:T(8,128)} %est_hbm.1, bf16[1,16,8,2048]{3,2,1,0:T(8,128)(2,1)} %cam_hbm.1, s32[1,512]{1,0:T(1,128)} %starts_hbm.1, s32[1,64]{1,0:T(1,128)} %index_hbm.1, f32[9,2,16]{2,1,0:T(2,128)} %bitcast.3), custom_call_target="tpu_custom_call" | custom-call | flops 600000000 | bytes 4000000 | tf_op jit(solution)/shard_map/pallas_call | solution.py:391
  56.0 1.0 %copy.7 = f32[8,64,512]{2,1,0:T(8,128)} copy(f32[8,64,512]{2,1,0:T(8,128)S(1)} %shard_map.55) | data formatting | bytes 2097152
